TPU v7x, 512 devices: a whole 4x8x8 slice. The times are simulated.
512 devices in a mesh: dp: 8 (over y), feat: 64 (over x, z, core).
Axes of the slice: x: 4, y: 8, z: 8, core: 2. Of those that a mesh axis runs over, the one named last changes fastest.
Arguments:
- features: bfloat16 [8, 16384, 128], P('dp', None, 'feat'), may hold values from -6 to 6
- tile_weights: bfloat16 [8, 1536, 128, 128], P('dp', 'feat'), may hold values from -0.15625 to 0.15625
- tile_rows: int32 [8, 1536], P('dp', 'feat'), may hold values from 0 to 1
- tile_owners: int32 [8, 1536, 1], P('dp', 'feat'), may hold values from 0 to 63; in each aligned block of 24 rows (0 to 23, 24 to 47, ..., all dimensions but the last counted through in order) at most 2 rows name the same one
- tile_blocks: int32 [8, 1536], P('dp', 'feat'), may hold values from 0 to 1
- tile_counts: int32 [8, 64], P('dp', 'feat'), may hold values from 6 to 24, as said below
- cotangent: bfloat16 [8, 16384, 1024], P('dp', 'feat'), may hold values from -0.046875 to 0.046875
- w_self: bfloat16 [128, 1024], replicated, may hold values from -0.5 to 0.5
- w_neigh: bfloat16 [128, 1024], replicated, may hold values from -0.5 to 0.5
- bias: float32 [1024], replicated, may hold values from -4 to 4
Outputs:
- grad_self: float32 [128, 1024], P(None, 'feat')
- grad_neigh: float32 [128, 1024], P(None, 'feat')
- grad_bias: float32 [1024], P('feat')
Inputs may be any that keep to these rules, and one draw needn't show every extreme that they name: `tile_owners`: among the 24 tile slots of one device at most 2 name one owner, a bound that some block of them reaches. `tile_counts`: in every batch some device has all 24 slots live.
All inputs are finite; a program needn't handle non-finite values.
Results may differ from a plain program's by a relative error of at most 0.008.
Values may be sent and summed in bfloat16 or wider, within the bound.
No kernel may reach another device: no remote copies, remote signals or barrier semaphores. Data moves between devices by JAX's collectives and lax.ppermute only.
A program may use at most 64 MiB of HBM per device.

v0:
```python
import jax
import jax.numpy as jnp
from jax import lax
from jax.sharding import PartitionSpec as P


def silu_slope(pre_act):
    sigmoid_z = jax.nn.sigmoid(pre_act)
    return sigmoid_z * (1.0 + pre_act * (1.0 - sigmoid_z))


def local(
    features,
    tile_weights,
    tile_rows,
    tile_owners,
    tile_blocks,
    tile_counts,
    cotangent,
    w_self,
    w_neigh,
    bias,
):
    owned = lax.all_to_all(features, "feat", split_axis=1, concat_axis=2, tiled=True)[0]
    node_rows, feat_width = owned.shape
    slot_count = tile_weights.shape[1]
    tile_side = tile_weights.shape[2]
    row_blocks = node_rows // tile_side
    peer_count = lax.axis_size("feat")
    row_index = tile_rows[0]
    owner_index = tile_owners[0, :, 0]
    block_index = tile_blocks[0]
    live = jnp.arange(slot_count, dtype=jnp.int32) < tile_counts[0, 0]
    whole = lax.all_gather(owned, "feat", axis=0, tiled=True)
    picked = whole.reshape(-1, tile_side, feat_width)[owner_index * row_blocks + block_index]
    products = jnp.einsum(
        "kij,kjf->kif", tile_weights[0], picked, preferred_element_type=jnp.float32
    )
    select = (
        (row_index[None, :] == jnp.arange(row_blocks, dtype=jnp.int32)[:, None]) & live[None, :]
    ).astype(jnp.float32)
    summed = jnp.einsum("rk,kif->rif", select, products, precision=lax.Precision.HIGHEST)
    neighbour = summed.reshape(node_rows, feat_width).astype(jnp.bfloat16)
    pre_act = (
        jnp.dot(owned, w_self, preferred_element_type=jnp.float32)
        + jnp.dot(neighbour, w_neigh, preferred_element_type=jnp.float32)
        + bias
    )
    slope = (cotangent[0].astype(jnp.float32) * silu_slope(pre_act)).astype(jnp.bfloat16)
    grad_s = jnp.einsum("nf,nh->fh", owned, slope, preferred_element_type=jnp.float32)
    grad_n = jnp.einsum("nf,nh->fh", neighbour, slope, preferred_element_type=jnp.float32)
    grad_b = jnp.sum(slope.astype(jnp.float32), axis=0)
    total_s, total_n, total_b = lax.psum((grad_s, grad_n, grad_b), ("dp", "feat"))
    column_count = w_self.shape[1] // peer_count
    start = lax.axis_index("feat") * column_count
    out_s = lax.dynamic_slice_in_dim(total_s, start, column_count, 1)
    out_n = lax.dynamic_slice_in_dim(total_n, start, column_count, 1)
    out_b = lax.dynamic_slice_in_dim(total_b, start, column_count, 0)
    return (out_s, out_n, out_b)


def solution(mesh):
    return jax.shard_map(
        local,
        mesh=mesh,
        in_specs=(
            P("dp", None, "feat"),
            P("dp", "feat", None, None),
            P("dp", "feat"),
            P("dp", "feat", None),
            P("dp", "feat"),
            P("dp", "feat"),
            P("dp", "feat", None),
            P(),
            P(),
            P(),
        ),
        out_specs=(P(None, "feat"), P(None, "feat"), P("feat")),
        check_vma=False,
    )
```

profile of v0, /device:TPU:23, one launch (start us, length us, event | category | flops | bytes accessed | tf_op | source)
XLA Modules:
  0.0 554.2 jit_solution(6314317441695136422)
XLA Ops:
  7.2 0.0 copy-start
  7.2 0.0 all-gather.2.cloned.1.call-start
  7.2 15.4 %copy.26 = bf16[1,16384,2]{2,0,1:T(2,128)(2,1)} copy(bf16[1,16384,2]{1,2,0:T(2,128)(2,1)} %param.10) | data formatting | bytes 131072 | tf_op args[0]
  22.6 0.5 broadcast.52
  23.1 90.8 %reduce = bf16[16384,2]{1,0:T(8,128)(2,1)} reduce(bf16[16384,1,2]{2,1,0:T(2,128)(2,1)} %bitcast.51, bf16[]{:T(256)} %broadcast.52), dimensions={1}, to_apply=%bitcast.36.reduce_sub_computation | reduce | bytes 131074
  113.9 7.1 %reshape.61 = bf16[64,2,256]{2,1,0:T(2,128)(2,1)S(1)} reshape(bf16[16384,2]{1,0:T(8,128)(2,1)} %reduce) | data formatting | bytes 131072
  121.0 21.9 %all_to_all.15 = bf16[64,2,256]{2,1,0:T(2,128)(2,1)S(1)} all-to-all(bf16[64,2,256]{2,1,0:T(2,128)(2,1)S(1)} %reshape.61), channel_id=1, replica_groups=mesh['dp'=8,'feat'=64] {'feat'}, dimensions={0} | all-to-all | bytes 131072 | tf_op jit(solution)/shard_map/all_to_all | solution.py:24
  142.9 16.4 %reshape.62 = bf16[16384,1,2]{2,1,0:T(2,128)(2,1)} reshape(bf16[64,2,256]{2,1,0:T(2,128)(2,1)S(1)} %all_to_all.15) | data formatting | bytes 131072
  159.3 0.0 copy-start.5
  159.3 0.0 copy-start.6
  159.3 0.0 copy-start.2
  159.3 15.4 %copy.27 = bf16[1,16384,2]{1,2,0:T(2,128)(2,1)S(1)} copy(bf16[1,16384,2]{2,0,1:T(2,128)(2,1)} %bitcast.52) | data formatting | bytes 131072 | tf_op jit(solution)/shard_map/all_to_all | solution.py:24
  174.7 0.1 copy.28
  174.8 0.7 squeeze.14
  175.4 0.0 all-gather.2.cloned.1.call-update
  175.5 0.2 all-reduce.3.cloned.1.call-start
  176.3 0.0 copy-done.5
  176.4 0.0 copy-done.6
  176.4 0.0 copy-done.2
  176.4 1.2 fusion.10
  177.6 77.5 %all-gather.2.cloned.1.call-done = bf16[16384,128]{0,1:T(8,128)(2,1)} async-done(((bf16[256,128]{0,1:T(8,128)(2,1)}), bf16[16384,128]{0,1:T(8,128)(2,1)}) %all-gather.2.cloned.1.call-update) | async-done | bytes 4194320 | tf_op jit(solution)/shard_map/all_gather | solution.py:34
  255.0 6.4 %copy.29 = bf16[16384,128]{1,0:T(8,128)(2,1)} copy(bf16[16384,128]{0,1:T(8,128)(2,1)} %all-gather.2.cloned.1.call-done) | data formatting | bytes 8388608 | tf_op jit(solution)/shard_map/all_gather | solution.py:34
  261.4 0.0 copy-start.3
  261.4 2.9 gather_fusion
  264.3 0.0 copy-done
  264.4 0.0 copy-start.4
  264.4 1.9 convolution_bitcast_fusion
  266.2 2.0 copy.31
  268.2 0.0 copy-done.3
  268.2 0.6 convolution_convert_fusion
  268.8 0.0 copy-start.1
  268.8 0.0 copy-done.4
  268.9 1.8 convert_reduce_fusion
  270.6 1.1 fusion.11
  271.8 0.0 copy-done.1
  271.8 1.1 convolution_bitcast_fusion.1
  272.9 0.0 all-reduce.3.cloned.1.call-update
  272.9 96.3 %psum.23 = f32[1024]{0:T(1024)S(1)} all-reduce(f32[1024]{0:T(1024)S(1)} %get-tuple-element.5), channel_id=1, replica_groups=mesh['dp'=8,'feat'=64] {'dp','feat'}, use_global_device_ids=true, to_apply=%region_3.0 | all-reduce | flops 1024 | bytes 8192 | tf_op jit(solution)/shard_map/psum | solution.py:53
  369.3 0.6 dynamic_slice.11
  369.9 176.2 %all-reduce.3.cloned.1.call-done = (f32[128,1024]{0,1:T(8,128)}, f32[128,1024]{0,1:T(8,128)}) async-done(((f32[128,1024]{0,1:T(8,128)}, f32[128,1024]{0,1:T(8,128)}), (f32[128,1024]{0,1:T(8,128)}, f32[128,1024]{0,1:T(8,128)})) %all-reduce.3.cloned.1.call-update) | async-done | bytes 1048592 | tf_op jit(solution)/shard_map/psum | solution.py:53
  546.0 1.3 constant_dynamic-slice_fusion
  (5 shorter events, 0.0 us)
Async XLA Ops:
  7.2 257.2 %copy-start = (bf16[1,24,128,128]{3,2,1,0:T(8,128)(2,1)S(1)}, bf16[1,24,128,128]{3,2,1,0:T(8,128)(2,1)}, u32[]{:S(2)}) copy-start(bf16[1,24,128,128]{3,2,1,0:T(8,128)(2,1)} %param.11) | copy-start | bytes 2359300
  7.2 247.8 %all-gather.2.cloned.1.call-start = ((), (), s32[]{:S(2)}) async-start(), calls=%async_computation.1 | async-start | bytes 4259840 | tf_op jit(solution)/shard_map/all_gather | solution.py:34
  159.3 17.1 %copy-start.5 = (s32[1,24]{1,0:T(1,128)S(1)}, s32[1,24]{1,0:T(1,128)}, u32[]{:S(2)}) copy-start(s32[1,24]{1,0:T(1,128)} %param.14) | copy-start | bytes 292
  159.3 17.1 %copy-start.6 = (s32[1,24,1]{1,2,0:T(1,128)S(1)}, s32[1,24,1]{1,2,0:T(1,128)}, u32[]{:S(2)}) copy-start(s32[1,24,1]{1,2,0:T(1,128)} %param.13) | copy-start | bytes 292
  159.3 17.1 %copy-start.2 = (bf16[128,1024]{1,0:T(8,128)(2,1)S(1)}, bf16[128,1024]{1,0:T(8,128)(2,1)}, u32[]{:S(2)}) copy-start(bf16[128,1024]{1,0:T(8,128)(2,1)} %param.17) | copy-start | bytes 786436
  175.5 370.6 %all-reduce.3.cloned.1.call-start = ((), (), s32[]{:S(2)}) async-start(), calls=%async_computation.2 | async-start | bytes 2097152 | tf_op jit(solution)/shard_map/psum | solution.py:53
  261.4 6.8 %copy-start.3 = (s32[1,24]{1,0:T(1,128)S(1)}, s32[1,24]{1,0:T(1,128)}, u32[]{:S(2)}) copy-start(s32[1,24]{1,0:T(1,128)} %param.12) | copy-start | bytes 292
  264.4 4.5 copy-start.4
  268.8 3.0 copy-start.1
Sparse Core Ops, SparseCore 0:
  175.6 79.3 all-gather.1
  273.1 272.9 all-reduce.2
where the time goes:
time: 556 us; the launch traced here: 554 us
  waiting for transfers between devices  254 us (46%)
  blocking collectives  118 us (21%)
  other arithmetic  90.8 us (16%)
  local copies, waits for them, and re-layouts  68.7 us (12%)
  between operations  14.9 us (3%)
  matrix products  7.67 us (1%)
    psum x1, waiting for transfers between devices, local(): lax.psum((grad_s, grad_n, grad_b), ('dp', 'feat'))  176 us
    psum x1, blocking collectives, local(): lax.psum((grad_s, grad_n, grad_b), ('dp', 'feat'))  96.3 us
    unnamed x1, other arithmetic  90.8 us
    all_gather x1, waiting for transfers between devices, local(): whole = lax.all_gather(owned, 'feat', axis=0, tiled=True)  77.5 us
    unnamed x19, local copies, waits for them, and re-layouts  39.5 us
    all_to_all x1, blocking collectives, local(): lax.all_to_all(features, 'feat', split_axis=1, concat_axis=2, tiled=True)[0]  21.9 us
    all_to_all x2, local copies, waits for them, and re-layouts, local(): lax.all_to_all(features, 'feat', split_axis=1, concat_axis=2, tiled=True)[0]  15.5 us
  transfers between devices with their start and end apart: 2, of which 2 were waited for; matrix products, arithmetic and copies ran while one was open for 0% of the time, Pallas kernels for 0%

commit v1 on v0

--- a/solution.py
+++ b/solution.py
@@ -21,7 +21,10 @@
     w_neigh,
     bias,
 ):
-    owned = lax.all_to_all(features, "feat", split_axis=1, concat_axis=2, tiled=True)[0]
+    owned = jnp.concatenate(
+        lax.all_to_all(jnp.stack(jnp.split(features, lax.axis_size("feat"), axis=1)), "feat", 0, 0),
+        axis=2,
+    )[0]
     node_rows, feat_width = owned.shape
     slot_count = tile_weights.shape[1]
     tile_side = tile_weights.shape[2]

time: 556 us -> 447 us (0.80)
  other arithmetic: 90.8 us -> 0.69 us
  local copies, waits for them, and re-layouts: 68.7 us -> 52 us
    unnamed x1 -> x0, other arithmetic: 90.8 us -> none
    all_to_all x2 -> x0, local copies, waits for them, and re-layouts: 15.5 us -> none  [local(): lax.all_to_all(features, 'feat', split_axis=1, concat_axis=2, tiled=True)[0]]
    all_gather x1 -> x0, local copies, waits for them, and re-layouts: 6.42 us -> none  [local(): whole = lax.all_gather(owned, 'feat', axis=0, tiled=True)]
    unnamed x19 -> x73, local copies, waits for them, and re-layouts: 39.5 us -> 43.8 us
  transfers between devices with their start and end apart: 2 -> 2, of which waited for: 2 -> 2; matrix products, arithmetic and copies ran while one was open for 0% -> 1% of each run, Pallas kernels for 0% -> 0%
where the time goes in v1:
time: 447 us; the launch traced here: 446 us
  waiting for transfers between devices  253 us (57%)
  blocking collectives  119 us (27%)
  local copies, waits for them, and re-layouts  52 us (12%)
  between operations  14.8 us (3%)
  matrix products  6.66 us (1%)
    psum x1, waiting for transfers between devices, local(): lax.psum((grad_s, grad_n, grad_b), ('dp', 'feat'))  175 us
    psum x1, blocking collectives, local(): lax.psum((grad_s, grad_n, grad_b), ('dp', 'feat'))  96.7 us
    all_gather x1, waiting for transfers between devices, local(): whole = lax.all_gather(owned, 'feat', axis=0, tiled=True)  78.2 us
    unnamed x73, local copies, waits for them, and re-layouts  43.8 us
    all_to_all x1, blocking collectives, local(): lax.all_to_all(jnp.stack(jnp.split(features, lax.axis_size('feat'), axis=...  21.9 us
  transfers between devices with their start and end apart: 2, of which 2 were waited for; matrix products, arithmetic and copies ran while one was open for 1% of the time, Pallas kernels for 0%

profile of v1, /device:TPU:23, one launch (start us, length us, event | category | flops | bytes accessed | tf_op | source)
XLA Modules:
  0.0 445.6 jit_solution(4177702184545146926)
XLA Ops:
  7.2 0.7 constant_dynamic-update-slice_fusion.63
  8.0 0.7 constant_dynamic-update-slice_fusion.62
  8.7 0.7 constant_dynamic-update-slice_fusion.61
  9.3 0.7 constant_dynamic-update-slice_fusion.60
  10.0 0.7 constant_dynamic-update-slice_fusion.59
  10.7 0.7 constant_dynamic-update-slice_fusion.58
  11.4 0.7 constant_dynamic-update-slice_fusion.57
  12.1 0.7 constant_dynamic-update-slice_fusion.56
  12.8 0.7 constant_dynamic-update-slice_fusion.55
  13.5 0.7 constant_dynamic-update-slice_fusion.54
  14.2 0.7 constant_dynamic-update-slice_fusion.53
  14.9 0.7 constant_dynamic-update-slice_fusion.52
  15.5 0.7 constant_dynamic-update-slice_fusion.51
  16.2 0.7 constant_dynamic-update-slice_fusion.50
  16.9 0.7 constant_dynamic-update-slice_fusion.49
  17.6 0.7 constant_dynamic-update-slice_fusion.48
  18.3 0.7 constant_dynamic-update-slice_fusion.47
  19.7 0.7 constant_dynamic-update-slice_fusion.45
  20.4 0.7 constant_dynamic-update-slice_fusion.44
  22.4 0.7 constant_dynamic-update-slice_fusion.41
  25.2 0.7 constant_dynamic-update-slice_fusion.37
  27.2 0.7 constant_dynamic-update-slice_fusion.34
  27.9 0.7 constant_dynamic-update-slice_fusion.33
  30.0 0.7 constant_dynamic-update-slice_fusion.30
  30.7 0.7 constant_dynamic-update-slice_fusion.29
  32.7 0.7 constant_dynamic-update-slice_fusion.26
  33.4 0.7 constant_dynamic-update-slice_fusion.25
  35.5 0.7 constant_dynamic-update-slice_fusion.22
  38.2 0.7 constant_dynamic-update-slice_fusion.18
  40.3 0.7 constant_dynamic-update-slice_fusion.15
  41.0 0.7 constant_dynamic-update-slice_fusion.14
  43.1 0.7 constant_dynamic-update-slice_fusion.11
  43.7 0.7 constant_dynamic-update-slice_fusion.10
  45.8 0.7 constant_dynamic-update-slice_fusion.7
  46.5 0.7 constant_dynamic-update-slice_fusion.6
  48.6 0.7 constant_dynamic-update-slice_fusion.3
  51.3 21.9 %all_to_all.5 = bf16[64,1,256,2]{2,3,1,0:T(2,128)(2,1)S(1)} all-to-all(bf16[64,1,256,2]{2,3,1,0:T(2,128)(2,1)S(1)} %constant_dynamic-update-slice_fusion), channel_id=1, replica_groups=mesh['dp'=8,'feat'=64] {'feat'}, dimensions={0} | all-to-all | bytes 131072 | tf_op jit(solution)/shard_map/all_to_all | solution.py:25
  73.2 0.7 copy.13
  75.4 1.3 fusion.16
  76.6 78.2 %all-gather.2.cloned.1.call-done = bf16[16384,128]{1,0:T(8,128)(2,1)} async-done(((bf16[256,128]{1,0:T(8,128)(2,1)}), bf16[16384,128]{1,0:T(8,128)(2,1)}) %all-gather.2.cloned.1.call-update) | async-done | bytes 4194320 | tf_op jit(solution)/shard_map/all_gather | solution.py:37
  154.8 2.9 gather_fusion
  157.7 1.9 fusion.7
  159.6 2.0 copy.15
  163.3 1.1 fusion.18
  164.5 1.1 fusion.17
  165.6 96.7 %psum.23 = f32[1024]{0:T(1024)S(1)} all-reduce(f32[1024]{0:T(1024)S(1)} %get-tuple-element.5), channel_id=1, replica_groups=mesh['dp'=8,'feat'=64] {'dp','feat'}, use_global_device_ids=true, to_apply=%region_3.0 | all-reduce | flops 1024 | bytes 8192 | tf_op jit(solution)/shard_map/psum | solution.py:56
  262.9 174.5 %all-reduce.3.cloned.1.call-done = (f32[128,1024]{0,1:T(8,128)}, f32[128,1024]{0,1:T(8,128)}) async-done(((f32[128,1024]{0,1:T(8,128)}, f32[128,1024]{0,1:T(8,128)}), (f32[128,1024]{0,1:T(8,128)}, f32[128,1024]{0,1:T(8,128)})) %all-reduce.3.cloned.1.call-update) | async-done | bytes 1048592 | tf_op jit(solution)/shard_map/psum | solution.py:56
  437.4 1.3 constant_dynamic-slice_fusion
  (50 shorter events, 22.4 us)
Async XLA Ops:
  7.2 150.6 %copy-start = (bf16[1,24,128,128]{3,2,1,0:T(8,128)(2,1)S(1)}, bf16[1,24,128,128]{3,2,1,0:T(8,128)(2,1)}, u32[]{:S(2)}) copy-start(bf16[1,24,128,128]{3,2,1,0:T(8,128)(2,1)} %param.11) | copy-start | bytes 2359300
  7.2 147.7 %all-gather.2.cloned.1.call-start = ((), (), s32[]{:S(2)}) async-start(), calls=%async_computation.1 | async-start | bytes 4259840 | tf_op jit(solution)/shard_map/all_gather | solution.py:37
  74.0 363.5 %all-reduce.3.cloned.1.call-start = ((), (), s32[]{:S(2)}) async-start(), calls=%async_computation.2 | async-start | bytes 2097152 | tf_op jit(solution)/shard_map/psum | solution.py:56
  159.6 2.0 copy-start.1
  161.6 1.0 copy-start.2
  161.6 1.1 copy-start.3
  161.6 1.1 copy-start.4
Sparse Core Ops, SparseCore 0:
  74.1 80.7 all-gather.1
  165.8 271.6 all-reduce.2
